TPU v7x, 256 devices: a whole 4x4x8 slice. The times are simulated.
256 devices in a mesh: sec: 16 (over x_hi, y, core), seq: 16 (over z, x_lo).
Axes of the slice: x: 4 (x_hi: 2, x_lo: 2; x = x_hi * 2 + x_lo), y: 4, z: 8, core: 2. Of those that a mesh axis runs over, the one named last changes fastest.
Arguments:
- stream: bfloat16 [512, 2048], replicated, may hold values from -6 to 6
- norm_gain: float32 [16, 2048], P('sec'), may hold values from 0.1 to 1.9
- qkv_weight: bfloat16 [16, 2048, 6144], P('sec', None, 'seq'), may hold values from -0.125 to 0.125
- out_weight: bfloat16 [16, 2048, 2048], P('sec', 'seq'), may hold values from -0.375 to 0.375
- stale_kv: bfloat16 [16, 512, 16, 256], P('sec', None, 'seq'), may hold values from -128 to 128, as said below
Outputs:
- section_out: bfloat16 [16, 512, 2048], P('sec', 'seq')
- fresh_kv: bfloat16 [16, 512, 16, 256], P('sec', None, 'seq')
Inputs may be any that keep to these rules, and one draw needn't show every extreme that they name: `stale_kv`: the last 128 entries of each head (values) are of order one; keys may carry a larger scale per token.
All inputs are finite; a program needn't handle non-finite values.
Results may differ from a plain program's by a relative error of at most 0.04.
Values may be sent and summed in bfloat16 or wider, within the bound.
A program may use at most 64 MiB of HBM per device.

v0:
```python
import math

import jax
import jax.numpy as jnp
from jax import lax
from jax.sharding import PartitionSpec as P

PATCHES = 4
ROWS = 8


def from_behind(value, axis, by):
    devices = lax.axis_size(axis)
    pairs = [(i, i + by) for i in range(devices) if 0 <= i + by < devices]
    return lax.ppermute(value, axis, pairs)


def on_device(stream, norm_gain, qkv_weight, out_weight, stale_kv):
    gain = norm_gain[0]
    weight_qkv = qkv_weight[0]
    weight_out = out_weight[0]
    stale = stale_kv[0]
    width = stream.shape[1]
    share = stale.shape[1]
    head_size = stale.shape[2] // 2
    seq_count = lax.axis_size("seq")
    patch_rows = seq_count * ROWS
    scale = 1.0 / math.sqrt(head_size)
    sec_pos = lax.axis_index("sec")
    seq_pos = lax.axis_index("seq")
    step_count = lax.axis_size("sec") + PATCHES - 1
    stale_five = stale.reshape(seq_count, PATCHES, ROWS, share, 2 * head_size)
    stale_keys = stale_five[..., :head_size]
    stale_vals = stale_five[..., head_size:]
    patch_ids = jnp.arange(PATCHES)
    same_shard = jnp.eye(seq_count, dtype=bool)
    stream_four = stream.reshape(seq_count, PATCHES, ROWS, width)

    def normalize(x_rows):
        x_float = x_rows.astype(jnp.float32)
        meansq = jnp.mean(x_float * x_float, axis=-1, keepdims=True)
        return (x_float * lax.rsqrt(meansq + 1e-06) * gain).astype(jnp.bfloat16)

    def project(piece):
        return jnp.dot(piece, weight_qkv, preferred_element_type=jnp.float32).astype(jnp.bfloat16)

    def step_fn(step_index, carry):
        incoming, fresh, result = carry
        patch_now = step_index - sec_pos
        active = (patch_now >= 0) & (patch_now < PATCHES)
        patch_clip = jnp.clip(patch_now, 0, PATCHES - 1)
        local_patch = lax.dynamic_index_in_dim(stream_four, patch_clip, 1, keepdims=False)
        x_whole = jnp.where(sec_pos == 0, local_patch.reshape(patch_rows, width), incoming)
        x_rows = lax.dynamic_slice_in_dim(x_whole, seq_pos * ROWS, ROWS, 0)
        projected = project(normalize(x_whole))
        projected = projected.reshape(seq_count, ROWS, share, 3, head_size)
        query = projected[..., 0, :]
        kv_new = jnp.concatenate([projected[..., 1, :], projected[..., 2, :]], axis=-1)
        updated = lax.dynamic_update_index_in_dim(fresh, kv_new, patch_clip, 1)
        key_mask = same_shard[:, :, None] & (patch_ids <= patch_now)[None, None, :]
        wide_mask = key_mask[:, None, None, :, :, None]
        s_stale = (
            jnp.einsum("irhd,jpkhd->irhjpk", query, stale_keys, preferred_element_type=jnp.float32)
            * scale
        )
        s_fresh = (
            jnp.einsum(
                "irhd,jpkhd->irhjpk",
                query,
                updated[..., :head_size],
                preferred_element_type=jnp.float32,
            )
            * scale
        )
        scores = jnp.where(wide_mask, s_fresh, s_stale)
        peak = jnp.max(scores, axis=(3, 4, 5))
        expo = jnp.exp(scores - peak[..., None, None, None])
        total = jnp.sum(expo, axis=(3, 4, 5))
        weights = (expo / total[..., None, None, None]).astype(jnp.bfloat16)
        zero = jnp.zeros((), jnp.bfloat16)
        context = jnp.einsum(
            "irhjpk,jpkhd->irhd",
            jnp.where(wide_mask, weights, zero),
            updated[..., head_size:],
            preferred_element_type=jnp.float32,
        )
        context = context + jnp.einsum(
            "irhjpk,jpkhd->irhd",
            jnp.where(wide_mask, zero, weights),
            stale_vals,
            preferred_element_type=jnp.float32,
        )
        context = context.astype(jnp.bfloat16).reshape(patch_rows, share * head_size)
        summed = lax.psum_scatter(
            jnp.dot(context, weight_out, preferred_element_type=jnp.float32).astype(jnp.bfloat16),
            "seq",
            scatter_dimension=0,
            tiled=True,
        ).astype(jnp.float32)
        output_rows = (summed + x_rows.astype(jnp.float32)).astype(jnp.bfloat16)
        next_fresh = jnp.where(active, updated, fresh)
        placed = lax.dynamic_update_slice_in_dim(result, output_rows, patch_clip * ROWS, 0)
        next_result = jnp.where(active, placed, result)
        whole_out = lax.all_gather(output_rows, "seq", axis=0, tiled=True)
        received = from_behind(whole_out, "sec", 1)
        return (received, next_fresh, next_result)

    init_in = jnp.zeros((patch_rows, width), jnp.bfloat16)
    init_fresh = jnp.zeros_like(stale_five)
    init_result = jnp.zeros((PATCHES * ROWS, width), jnp.bfloat16)
    final = lax.fori_loop(0, step_count, step_fn, (init_in, init_fresh, init_result))
    return (final[2][None], final[1].reshape(-1, share, 2 * head_size)[None])


def solution(mesh):
    return jax.shard_map(
        on_device,
        mesh=mesh,
        in_specs=(
            P(),
            P("sec", None),
            P("sec", None, "seq"),
            P("sec", "seq", None),
            P("sec", None, "seq", None),
        ),
        out_specs=(P("sec", "seq", None), P("sec", None, "seq", None)),
        check_vma=False,
    )
```

profile of v0, /device:TPU:255, one launch (start us, length us, event | category | flops | bytes accessed | tf_op | source)
XLA Modules:
  0.0 2362.1 jit_solution(7353288488879758919)
XLA Ops:
  8.4 2346.5 %while.20 = (s32[]{:T(128)}, bf16[128,2048]{1,0:T(8,128)(2,1)S(1)}, bf16[16,4,8,1,256]{4,2,1,0,3:T(8,128)(2,1)S(1)}, bf16[32,2048]{1,0:T(8,128)(2,1)S(1)}, pred[...) while((s32[]{:T(128)}, bf16[128,2048]{1,0:T(8,128)(2,1)S(1)}, ...), condition=%wide.region_5.6_spmd.clone, body=%wide.region_0.5_spmd.clone.sunk | while | flops 339313792 | bytes 16474538 | solution.py:111
  15.9 55.8 %reduce-scatter.2.cloned.1.call-done = bf16[8,2048]{1,0:T(8,128)(2,1)} async-done(((bf16[128,2048]{1,0:T(8,128)(2,1)}), bf16[8,2048]{1,0:T(8,128)(2,1)}) %reduce-scatter.2.cloned.1.call-update) | async-done | bytes 32784 | tf_op jit(solution)/shard_map/while/body/eval_jaxpr/reduce_scatter | solution.py:94
  72.4 28.0 %all_gather.11 = bf16[128,2048]{1,0:T(8,128)(2,1)S(1)} all-gather(bf16[8,2048]{1,0:T(8,128)(2,1)S(1)} %get-tuple-element.535), channel_id=1, replica_groups=mesh['sec'=16,'seq'=16] {'seq'}, dimensions={0}, use_global_device_ids=true | all-gather | bytes 557056 | tf_op jit(solution)/shard_map/while/body/eval_jaxpr/all_gather | solution.py:104
  129.5 66.4 %reduce-scatter.2.cloned.1.call-done = bf16[8,2048]{1,0:T(8,128)(2,1)} async-done(((bf16[128,2048]{1,0:T(8,128)(2,1)}), bf16[8,2048]{1,0:T(8,128)(2,1)}) %reduce-scatter.2.cloned.1.call-update) | async-done | bytes 32784 | tf_op jit(solution)/shard_map/while/body/eval_jaxpr/reduce_scatter | solution.py:94
  253.1 66.7 %reduce-scatter.2.cloned.1.call-done = bf16[8,2048]{1,0:T(8,128)(2,1)} async-done(((bf16[128,2048]{1,0:T(8,128)(2,1)}), bf16[8,2048]{1,0:T(8,128)(2,1)}) %reduce-scatter.2.cloned.1.call-update) | async-done | bytes 32784 | tf_op jit(solution)/shard_map/while/body/eval_jaxpr/reduce_scatter | solution.py:94
  377.8 67.0 %reduce-scatter.2.cloned.1.call-done = bf16[8,2048]{1,0:T(8,128)(2,1)} async-done(((bf16[128,2048]{1,0:T(8,128)(2,1)}), bf16[8,2048]{1,0:T(8,128)(2,1)}) %reduce-scatter.2.cloned.1.call-update) | async-done | bytes 32784 | tf_op jit(solution)/shard_map/while/body/eval_jaxpr/reduce_scatter | solution.py:94
  501.4 67.0 %reduce-scatter.2.cloned.1.call-done = bf16[8,2048]{1,0:T(8,128)(2,1)} async-done(((bf16[128,2048]{1,0:T(8,128)(2,1)}), bf16[8,2048]{1,0:T(8,128)(2,1)}) %reduce-scatter.2.cloned.1.call-update) | async-done | bytes 32784 | tf_op jit(solution)/shard_map/while/body/eval_jaxpr/reduce_scatter | solution.py:94
  569.1 27.7 %all_gather.11 = bf16[128,2048]{1,0:T(8,128)(2,1)S(1)} all-gather(bf16[8,2048]{1,0:T(8,128)(2,1)S(1)} %get-tuple-element.535), channel_id=1, replica_groups=mesh['sec'=16,'seq'=16] {'seq'}, dimensions={0}, use_global_device_ids=true | all-gather | bytes 557056 | tf_op jit(solution)/shard_map/while/body/eval_jaxpr/all_gather | solution.py:104
  625.6 66.6 %reduce-scatter.2.cloned.1.call-done = bf16[8,2048]{1,0:T(8,128)(2,1)} async-done(((bf16[128,2048]{1,0:T(8,128)(2,1)}), bf16[8,2048]{1,0:T(8,128)(2,1)}) %reduce-scatter.2.cloned.1.call-update) | async-done | bytes 32784 | tf_op jit(solution)/shard_map/while/body/eval_jaxpr/reduce_scatter | solution.py:94
  750.2 66.5 %reduce-scatter.2.cloned.1.call-done = bf16[8,2048]{1,0:T(8,128)(2,1)} async-done(((bf16[128,2048]{1,0:T(8,128)(2,1)}), bf16[8,2048]{1,0:T(8,128)(2,1)}) %reduce-scatter.2.cloned.1.call-update) | async-done | bytes 32784 | tf_op jit(solution)/shard_map/while/body/eval_jaxpr/reduce_scatter | solution.py:94
  873.9 66.8 %reduce-scatter.2.cloned.1.call-done = bf16[8,2048]{1,0:T(8,128)(2,1)} async-done(((bf16[128,2048]{1,0:T(8,128)(2,1)}), bf16[8,2048]{1,0:T(8,128)(2,1)}) %reduce-scatter.2.cloned.1.call-update) | async-done | bytes 32784 | tf_op jit(solution)/shard_map/while/body/eval_jaxpr/reduce_scatter | solution.py:94
  997.7 66.8 %reduce-scatter.2.cloned.1.call-done = bf16[8,2048]{1,0:T(8,128)(2,1)} async-done(((bf16[128,2048]{1,0:T(8,128)(2,1)}), bf16[8,2048]{1,0:T(8,128)(2,1)}) %reduce-scatter.2.cloned.1.call-update) | async-done | bytes 32784 | tf_op jit(solution)/shard_map/while/body/eval_jaxpr/reduce_scatter | solution.py:94
  1121.7 66.8 %reduce-scatter.2.cloned.1.call-done = bf16[8,2048]{1,0:T(8,128)(2,1)} async-done(((bf16[128,2048]{1,0:T(8,128)(2,1)}), bf16[8,2048]{1,0:T(8,128)(2,1)}) %reduce-scatter.2.cloned.1.call-update) | async-done | bytes 32784 | tf_op jit(solution)/shard_map/while/body/eval_jaxpr/reduce_scatter | solution.py:94
  1245.9 66.5 %reduce-scatter.2.cloned.1.call-done = bf16[8,2048]{1,0:T(8,128)(2,1)} async-done(((bf16[128,2048]{1,0:T(8,128)(2,1)}), bf16[8,2048]{1,0:T(8,128)(2,1)}) %reduce-scatter.2.cloned.1.call-update) | async-done | bytes 32784 | tf_op jit(solution)/shard_map/while/body/eval_jaxpr/reduce_scatter | solution.py:94
  1369.5 66.9 %reduce-scatter.2.cloned.1.call-done = bf16[8,2048]{1,0:T(8,128)(2,1)} async-done(((bf16[128,2048]{1,0:T(8,128)(2,1)}), bf16[8,2048]{1,0:T(8,128)(2,1)}) %reduce-scatter.2.cloned.1.call-update) | async-done | bytes 32784 | tf_op jit(solution)/shard_map/while/body/eval_jaxpr/reduce_scatter | solution.py:94
  1493.7 66.0 %reduce-scatter.2.cloned.1.call-done = bf16[8,2048]{1,0:T(8,128)(2,1)} async-done(((bf16[128,2048]{1,0:T(8,128)(2,1)}), bf16[8,2048]{1,0:T(8,128)(2,1)}) %reduce-scatter.2.cloned.1.call-update) | async-done | bytes 32784 | tf_op jit(solution)/shard_map/while/body/eval_jaxpr/reduce_scatter | solution.py:94
  1560.5 27.7 %all_gather.11 = bf16[128,2048]{1,0:T(8,128)(2,1)S(1)} all-gather(bf16[8,2048]{1,0:T(8,128)(2,1)S(1)} %get-tuple-element.535), channel_id=1, replica_groups=mesh['sec'=16,'seq'=16] {'seq'}, dimensions={0}, use_global_device_ids=true | all-gather | bytes 557056 | tf_op jit(solution)/shard_map/while/body/eval_jaxpr/all_gather | solution.py:104
  1617.9 66.4 %reduce-scatter.2.cloned.1.call-done = bf16[8,2048]{1,0:T(8,128)(2,1)} async-done(((bf16[128,2048]{1,0:T(8,128)(2,1)}), bf16[8,2048]{1,0:T(8,128)(2,1)}) %reduce-scatter.2.cloned.1.call-update) | async-done | bytes 32784 | tf_op jit(solution)/shard_map/while/body/eval_jaxpr/reduce_scatter | solution.py:94
  1741.3 66.8 %reduce-scatter.2.cloned.1.call-done = bf16[8,2048]{1,0:T(8,128)(2,1)} async-done(((bf16[128,2048]{1,0:T(8,128)(2,1)}), bf16[8,2048]{1,0:T(8,128)(2,1)}) %reduce-scatter.2.cloned.1.call-update) | async-done | bytes 32784 | tf_op jit(solution)/shard_map/while/body/eval_jaxpr/reduce_scatter | solution.py:94
  1808.8 27.9 %all_gather.11 = bf16[128,2048]{1,0:T(8,128)(2,1)S(1)} all-gather(bf16[8,2048]{1,0:T(8,128)(2,1)S(1)} %get-tuple-element.535), channel_id=1, replica_groups=mesh['sec'=16,'seq'=16] {'seq'}, dimensions={0}, use_global_device_ids=true | all-gather | bytes 557056 | tf_op jit(solution)/shard_map/while/body/eval_jaxpr/all_gather | solution.py:104
  1866.0 66.6 %reduce-scatter.2.cloned.1.call-done = bf16[8,2048]{1,0:T(8,128)(2,1)} async-done(((bf16[128,2048]{1,0:T(8,128)(2,1)}), bf16[8,2048]{1,0:T(8,128)(2,1)}) %reduce-scatter.2.cloned.1.call-update) | async-done | bytes 32784 | tf_op jit(solution)/shard_map/while/body/eval_jaxpr/reduce_scatter | solution.py:94
  1990.0 66.5 %reduce-scatter.2.cloned.1.call-done = bf16[8,2048]{1,0:T(8,128)(2,1)} async-done(((bf16[128,2048]{1,0:T(8,128)(2,1)}), bf16[8,2048]{1,0:T(8,128)(2,1)}) %reduce-scatter.2.cloned.1.call-update) | async-done | bytes 32784 | tf_op jit(solution)/shard_map/while/body/eval_jaxpr/reduce_scatter | solution.py:94
  2113.9 66.6 %reduce-scatter.2.cloned.1.call-done = bf16[8,2048]{1,0:T(8,128)(2,1)} async-done(((bf16[128,2048]{1,0:T(8,128)(2,1)}), bf16[8,2048]{1,0:T(8,128)(2,1)}) %reduce-scatter.2.cloned.1.call-update) | async-done | bytes 32784 | tf_op jit(solution)/shard_map/while/body/eval_jaxpr/reduce_scatter | solution.py:94
  2237.6 66.8 %reduce-scatter.2.cloned.1.call-done = bf16[8,2048]{1,0:T(8,128)(2,1)} async-done(((bf16[128,2048]{1,0:T(8,128)(2,1)}), bf16[8,2048]{1,0:T(8,128)(2,1)}) %reduce-scatter.2.cloned.1.call-update) | async-done | bytes 32784 | tf_op jit(solution)/shard_map/while/body/eval_jaxpr/reduce_scatter | solution.py:94
  (481 shorter events, 979.1 us)
Async XLA Ops:
  8.4 63.3 %reduce-scatter.2.cloned.1.call-start = ((), (), s32[]{:S(2)}) async-start(), calls=%async_computation.1 | async-start | bytes 557056 | tf_op jit(solution)/shard_map/while/body/eval_jaxpr/reduce_scatter | solution.py:94
  122.1 73.8 %reduce-scatter.2.cloned.1.call-start = ((), (), s32[]{:S(2)}) async-start(), calls=%async_computation.1 | async-start | bytes 557056 | tf_op jit(solution)/shard_map/while/body/eval_jaxpr/reduce_scatter | solution.py:94
  245.7 74.1 %reduce-scatter.2.cloned.1.call-start = ((), (), s32[]{:S(2)}) async-start(), calls=%async_computation.1 | async-start | bytes 557056 | tf_op jit(solution)/shard_map/while/body/eval_jaxpr/reduce_scatter | solution.py:94
  348.0 22.4 collective-permute-start
  370.4 74.4 %reduce-scatter.2.cloned.1.call-start = ((), (), s32[]{:S(2)}) async-start(), calls=%async_computation.1 | async-start | bytes 557056 | tf_op jit(solution)/shard_map/while/body/eval_jaxpr/reduce_scatter | solution.py:94
  472.1 21.9 collective-permute-start
  494.0 74.4 %reduce-scatter.2.cloned.1.call-start = ((), (), s32[]{:S(2)}) async-start(), calls=%async_computation.1 | async-start | bytes 557056 | tf_op jit(solution)/shard_map/while/body/eval_jaxpr/reduce_scatter | solution.py:94
  618.2 74.0 %reduce-scatter.2.cloned.1.call-start = ((), (), s32[]{:S(2)}) async-start(), calls=%async_computation.1 | async-start | bytes 557056 | tf_op jit(solution)/shard_map/while/body/eval_jaxpr/reduce_scatter | solution.py:94
  720.4 22.4 collective-permute-start
  742.8 73.9 %reduce-scatter.2.cloned.1.call-start = ((), (), s32[]{:S(2)}) async-start(), calls=%async_computation.1 | async-start | bytes 557056 | tf_op jit(solution)/shard_map/while/body/eval_jaxpr/reduce_scatter | solution.py:94
  866.5 74.2 %reduce-scatter.2.cloned.1.call-start = ((), (), s32[]{:S(2)}) async-start(), calls=%async_computation.1 | async-start | bytes 557056 | tf_op jit(solution)/shard_map/while/body/eval_jaxpr/reduce_scatter | solution.py:94
  990.3 74.2 %reduce-scatter.2.cloned.1.call-start = ((), (), s32[]{:S(2)}) async-start(), calls=%async_computation.1 | async-start | bytes 557056 | tf_op jit(solution)/shard_map/while/body/eval_jaxpr/reduce_scatter | solution.py:94
  1114.3 74.2 %reduce-scatter.2.cloned.1.call-start = ((), (), s32[]{:S(2)}) async-start(), calls=%async_computation.1 | async-start | bytes 557056 | tf_op jit(solution)/shard_map/while/body/eval_jaxpr/reduce_scatter | solution.py:94
  1238.4 73.9 %reduce-scatter.2.cloned.1.call-start = ((), (), s32[]{:S(2)}) async-start(), calls=%async_computation.1 | async-start | bytes 557056 | tf_op jit(solution)/shard_map/while/body/eval_jaxpr/reduce_scatter | solution.py:94
  1362.1 74.3 %reduce-scatter.2.cloned.1.call-start = ((), (), s32[]{:S(2)}) async-start(), calls=%async_computation.1 | async-start | bytes 557056 | tf_op jit(solution)/shard_map/while/body/eval_jaxpr/reduce_scatter | solution.py:94
  1486.3 73.4 %reduce-scatter.2.cloned.1.call-start = ((), (), s32[]{:S(2)}) async-start(), calls=%async_computation.1 | async-start | bytes 557056 | tf_op jit(solution)/shard_map/while/body/eval_jaxpr/reduce_scatter | solution.py:94
  1588.2 22.3 collective-permute-start
  1610.5 73.8 %reduce-scatter.2.cloned.1.call-start = ((), (), s32[]{:S(2)}) async-start(), calls=%async_computation.1 | async-start | bytes 557056 | tf_op jit(solution)/shard_map/while/body/eval_jaxpr/reduce_scatter | solution.py:94
  1733.9 74.2 %reduce-scatter.2.cloned.1.call-start = ((), (), s32[]{:S(2)}) async-start(), calls=%async_computation.1 | async-start | bytes 557056 | tf_op jit(solution)/shard_map/while/body/eval_jaxpr/reduce_scatter | solution.py:94
  1858.5 74.1 %reduce-scatter.2.cloned.1.call-start = ((), (), s32[]{:S(2)}) async-start(), calls=%async_computation.1 | async-start | bytes 557056 | tf_op jit(solution)/shard_map/while/body/eval_jaxpr/reduce_scatter | solution.py:94
  1982.6 73.9 %reduce-scatter.2.cloned.1.call-start = ((), (), s32[]{:S(2)}) async-start(), calls=%async_computation.1 | async-start | bytes 557056 | tf_op jit(solution)/shard_map/while/body/eval_jaxpr/reduce_scatter | solution.py:94
  2106.5 74.0 %reduce-scatter.2.cloned.1.call-start = ((), (), s32[]{:S(2)}) async-start(), calls=%async_computation.1 | async-start | bytes 557056 | tf_op jit(solution)/shard_map/while/body/eval_jaxpr/reduce_scatter | solution.py:94
  2230.2 74.2 %reduce-scatter.2.cloned.1.call-start = ((), (), s32[]{:S(2)}) async-start(), calls=%async_computation.1 | async-start | bytes 557056 | tf_op jit(solution)/shard_map/while/body/eval_jaxpr/reduce_scatter | solution.py:94
  2332.6 22.2 collective-permute-start
  (35 other events, 322.5 us)
Sparse Core Ops, SparseCore 0:
  16.0 55.6 reduce-scatter.1
  129.6 66.2 reduce-scatter.1
  253.3 66.5 reduce-scatter.1
  377.9 66.8 reduce-scatter.1
  501.5 66.7 reduce-scatter.1
  625.7 66.4 reduce-scatter.1
  750.3 66.3 reduce-scatter.1
  874.0 66.6 reduce-scatter.1
  997.8 66.6 reduce-scatter.1
  1121.8 66.6 reduce-scatter.1
  1246.0 66.3 reduce-scatter.1
  1369.7 66.7 reduce-scatter.1
  1493.8 65.8 reduce-scatter.1
  1618.0 66.2 reduce-scatter.1
  1741.4 66.6 reduce-scatter.1
  1866.1 66.4 reduce-scatter.1
  1990.1 66.3 reduce-scatter.1
  2114.0 66.4 reduce-scatter.1
  2237.7 66.6 reduce-scatter.1
where the time goes:
time: 2380 us; the launch traced here: 2360 us
  waiting for transfers between devices  1640 us (69%)
  blocking collectives  523 us (22%)
  matrix products  93.7 us (4%)
  other arithmetic  58.4 us (2%)
  starting transfers between devices  24.4 us (1%)
    reduce_scatter x19, waiting for transfers between devices, step_fn(): lax.psum_scatter(jnp.dot(context, weight_out, preferred_element_type=jnp....  1260 us
    all_gather x19, blocking collectives, step_fn(): whole_out = lax.all_gather(output_rows, 'seq', axis=0, tiled=True)  523 us
    ppermute x19, waiting for transfers between devices, from_behind(): return lax.ppermute(value, axis, pairs)  386 us
  transfers between devices with their start and end apart: 38, of which 38 were waited for; matrix products, arithmetic and copies ran while one was open for 0% of the time, Pallas kernels for 0%

commit v1 on v0

v1 whole, which is shorter than its diff:
```python
import functools
import math

import jax
import jax.numpy as jnp
from jax import lax
from jax.experimental import pallas as pl
from jax.experimental.pallas import tpu as pltpu
from jax.sharding import PartitionSpec as P

MESH = pl.DeviceIdType.MESH
SECS = 16
RING = 8
SEQS = 16
PATCHES = 4
ROWS = 8
SHARD = PATCHES * ROWS
CHUNK = 128
CHUNKS = 4
PER_CHUNK = CHUNK // SHARD
HEAD = 128
TILE = 256
EPS = 1e-06

GATHER = (
    ((1, 0), (0, 0)),
    ((-1, 0), (0, 0)),
    ((0, 1), (0, 0)),
    ((1, 0), (-1, 0)),
    ((-1, 0), (1, 0)),
    ((0, 1), (1, 0)),
    ((1, 0), (-2, 0)),
    ((-1, 0), (2, 0)),
    ((0, 1), (2, 0)),
    ((1, 0), (-3, 0)),
    ((-1, 0), (2, 1)),
    ((0, 1), (-2, 0)),
    ((1, 0), (-2, 1)),
    ((-1, 0), (3, 1)),
    ((0, 1), (-1, 0)),
)
Z_ORDER = (4, 3, -3, 2, -2, 1, -1, 0)


def slot(dz, dx):
    return (dz % RING) * 2 + dx % 2


def kernel(
    stream_ref,
    gain_ref,
    wqkv_ref,
    wout_ref,
    stale_ref,
    out_ref,
    fresh_ref,
    wfull,
    wqkv,
    gain,
    stale,
    ctx_in,
    x_in,
    x_cur,
    ctx_out,
    fresh,
    fin_in,
    fin_x,
    fin_out,
    load_sem,
    w_send,
    w_recv,
    own_send,
    ctx_send,
    ctx_recv,
    x_send,
    x_recv,
    fin_recv,
    finx_recv,
    out_send,
    out_recv,
    fresh_sem,
):
    s = lax.axis_index("sec")
    j = lax.axis_index("seq")
    z = j // 2
    xl = j % 2
    ahead = (s + 1) % SECS
    behind = (s + SECS - 1) % SECS
    width = wfull.shape[1]

    def place(dz, dx):
        return ((z + dz + RING) % RING) * 2 + (xl + dx) % 2

    loads = [
        pltpu.make_async_copy(wqkv_ref.at[0], wqkv, load_sem.at[0]),
        pltpu.make_async_copy(gain_ref, gain, load_sem.at[1]),
        pltpu.make_async_copy(stale_ref, stale, load_sem.at[2]),
    ]
    for load in loads:
        load.start()
    stream_load = pltpu.make_async_copy(stream_ref, x_cur, load_sem.at[3])

    @pl.when(s == 0)
    def _():
        stream_load.start()

    barrier = pltpu.get_barrier_semaphore()

    def greet(i, carry):
        pl.semaphore_signal(barrier, inc=1, device_id=(ahead, i), device_id_type=MESH)
        pl.semaphore_signal(barrier, inc=1, device_id=(behind, i), device_id_type=MESH)
        return carry

    lax.fori_loop(0, SEQS, greet, 0)
    for dz, dx in ((1, 0), (-1, 0), (0, 1)):
        pl.semaphore_signal(barrier, inc=1, device_id=(s, place(dz, dx)), device_id_type=MESH)
    pl.semaphore_wait(barrier, 2 * SEQS + 3)

    def block(index):
        return pl.ds(pl.multiple_of(index * HEAD, HEAD), HEAD)

    own = pltpu.make_async_remote_copy(
        src_ref=wout_ref.at[0],
        dst_ref=wfull.at[block(j), :],
        send_sem=own_send,
        recv_sem=w_recv.at[0],
        device_id=(ahead, j),
        device_id_type=MESH,
    )
    own.start()

    def wait_block(dz, dx):
        rows = block(place(dz, dx))
        pltpu.make_async_copy(
            wfull.at[rows, :], wfull.at[rows, :], w_recv.at[slot(dz, dx)]
        ).wait()

    def gather():
        arrived = set()

        def need(rel):
            if slot(*rel) not in arrived:
                arrived.add(slot(*rel))
                wait_block(*rel)

        sends = []
        for index, (step, rel) in enumerate(GATHER):
            need(rel)
            rows = block(place(*rel))
            send = pltpu.make_async_remote_copy(
                src_ref=wfull.at[rows, :],
                dst_ref=wfull.at[rows, :],
                send_sem=w_send.at[index],
                recv_sem=w_recv.at[slot(rel[0] - step[0], rel[1] + step[1])],
                device_id=(s, place(*step)),
                device_id_type=MESH,
            )
            send.start()
            sends.append(send)
        for dz in range(RING):
            for dx in range(2):
                need((dz, dx))
        for send in sends:
            send.wait_send()

    pl.when(s != 0)(gather)
    for load in loads:
        load.wait()

    @pl.when(s == 0)
    def _():
        stream_load.wait()

    scale = 1.0 / math.sqrt(HEAD)

    def wait_bytes(ref, sem):
        pltpu.make_async_copy(ref, ref, sem).wait()

    def process(c, carry):
        @pl.when(s != 0)
        def _():
            wait_bytes(ctx_in.at[c], ctx_recv.at[c])
            wait_bytes(x_in.at[c], x_recv.at[c])

            def columns(n, carry):
                cols = pl.ds(pl.multiple_of(n * TILE, TILE), TILE)
                lhs = jnp.concatenate([ctx_in[c, g] for g in range(SEQS)], axis=1)
                total = jnp.dot(lhs, wfull[:, cols], preferred_element_type=jnp.float32)
                total = total + x_in[c, :, cols].astype(jnp.float32)
                x_cur[c, :, cols] = total.astype(jnp.bfloat16)
                return carry

            lax.fori_loop(0, width // TILE, columns, 0)

        @pl.when(s != SECS - 1)
        def _():
            pltpu.make_async_remote_copy(
                src_ref=x_cur.at[c],
                dst_ref=x_in.at[c],
                send_sem=x_send.at[c],
                recv_sem=x_recv.at[c],
                device_id=(ahead, j),
                device_id_type=MESH,
            ).start()

        mine = c == j // PER_CHUNK
        my_rows = pl.ds(pl.multiple_of((j % PER_CHUNK) * SHARD, SHARD), SHARD)

        @pl.when(mine & (s == SECS - 1))
        def _():
            pltpu.make_async_remote_copy(
                src_ref=x_cur.at[c, my_rows, :],
                dst_ref=fin_x,
                send_sem=x_send.at[0],
                recv_sem=finx_recv,
                device_id=(ahead, j),
                device_id_type=MESH,
            ).start()

        @pl.when(mine & (s != 0))
        def _():
            pltpu.make_async_remote_copy(
                src_ref=x_cur.at[c, my_rows, :],
                dst_ref=out_ref.at[0],
                send_sem=out_send,
                recv_sem=out_recv,
                device_id=(behind, j),
                device_id_type=MESH,
            ).start()

        x = x_cur[c].astype(jnp.float32)
        meansq = jnp.mean(x * x, axis=-1, keepdims=True)
        normed = (x * lax.rsqrt(meansq + EPS) * gain[...]).astype(jnp.bfloat16)
        qkv = jnp.dot(normed, wqkv[...], preferred_element_type=jnp.float32).astype(jnp.bfloat16)
        query = qkv[:, :HEAD]
        key = qkv[:, HEAD : 2 * HEAD]
        value = qkv[:, 2 * HEAD :]
        tokens = pl.ds(pl.multiple_of(c * CHUNK, CHUNK), CHUNK)
        fresh[tokens, :] = qkv[:, HEAD:]
        pltpu.make_async_copy(
            fresh.at[tokens, :], fresh_ref.at[tokens, :], fresh_sem.at[c]
        ).start()

        contract = (((1,), (1,)), ((), ()))
        s_stale = (
            lax.dot_general(
                query, stale[:, :HEAD], contract, preferred_element_type=jnp.float32
            )
            * scale
        )
        s_fresh = (
            lax.dot_general(query, key, contract, preferred_element_type=jnp.float32) * scale
        )
        tokens_all = stale.shape[0]

        def is_fresh(count, first):
            row = lax.broadcasted_iota(jnp.int32, (CHUNK, count), 0) + c * CHUNK
            col = lax.broadcasted_iota(jnp.int32, (CHUNK, count), 1) + first
            same = (row >> 5) == (col >> 5)
            return same & (((col & 31) >> 3) <= ((row & 31) >> 3))

        low = -1e30
        s_stale = jnp.where(is_fresh(tokens_all, 0), low, s_stale)
        s_fresh = jnp.where(is_fresh(CHUNK, c * CHUNK), s_fresh, low)
        peak = jnp.maximum(
            jnp.max(s_stale, axis=1, keepdims=True), jnp.max(s_fresh, axis=1, keepdims=True)
        )
        e_stale = jnp.exp(s_stale - peak)
        e_fresh = jnp.exp(s_fresh - peak)
        norm = 1.0 / (
            jnp.sum(e_stale, axis=1, keepdims=True) + jnp.sum(e_fresh, axis=1, keepdims=True)
        )
        w_stale = (e_stale * norm).astype(jnp.bfloat16)
        w_fresh = (e_fresh * norm).astype(jnp.bfloat16)
        context = jnp.dot(w_stale, stale[:, HEAD:], preferred_element_type=jnp.float32)
        context = context + jnp.dot(w_fresh, value, preferred_element_type=jnp.float32)
        ctx_out[c] = context.astype(jnp.bfloat16)

        @pl.when(s != SECS - 1)
        def _():
            for dz in Z_ORDER:
                for dx in (1, 0):
                    pltpu.make_async_remote_copy(
                        src_ref=ctx_out.at[c],
                        dst_ref=ctx_in.at[c, j],
                        send_sem=ctx_send.at[c],
                        recv_sem=ctx_recv.at[c],
                        device_id=(ahead, place(dz, dx)),
                        device_id_type=MESH,
                    ).start()

        @pl.when(s == SECS - 1)
        def _():
            for i in range(PER_CHUNK):
                pltpu.make_async_remote_copy(
                    src_ref=ctx_out.at[c, pl.ds(i * SHARD, SHARD), :],
                    dst_ref=fin_in.at[j],
                    send_sem=ctx_send.at[c],
                    recv_sem=fin_recv,
                    device_id=(ahead, c * PER_CHUNK + i),
                    device_id_type=MESH,
                ).start()

        return carry

    lax.fori_loop(0, CHUNKS, process, 0)

    @pl.when(s == 0)
    def _():
        gather()
        wait_bytes(fin_in, fin_recv)
        wait_bytes(fin_x, finx_recv)

        def columns(n, carry):
            cols = pl.ds(pl.multiple_of(n * TILE, TILE), TILE)
            lhs = jnp.concatenate([fin_in[g] for g in range(SEQS)], axis=1)
            total = jnp.dot(lhs, wfull[:, cols], preferred_element_type=jnp.float32)
            total = total + fin_x[:, cols].astype(jnp.float32)
            fin_out[:, cols] = total.astype(jnp.bfloat16)
            return carry

        lax.fori_loop(0, width // TILE, columns, 0)
        pltpu.make_async_remote_copy(
            src_ref=fin_out,
            dst_ref=out_ref.at[0],
            send_sem=out_send,
            recv_sem=out_recv,
            device_id=(behind, j),
            device_id_type=MESH,
        ).start()

    own.wait_send()

    def drain(c, carry):
        tokens = pl.ds(pl.multiple_of(c * CHUNK, CHUNK), CHUNK)
        pltpu.make_async_copy(
            fresh.at[tokens, :], fresh_ref.at[tokens, :], fresh_sem.at[c]
        ).wait()

        @pl.when(s != SECS - 1)
        def _():
            wait_bytes(ctx_in.at[c], ctx_send.at[c])
            wait_bytes(x_in.at[c], x_send.at[c])

        @pl.when(s == SECS - 1)
        def _():
            wait_bytes(ctx_out.at[c], ctx_send.at[c])

        return carry

    lax.fori_loop(0, CHUNKS, drain, 0)

    @pl.when(s == SECS - 1)
    def _():
        wait_bytes(fin_x, x_send.at[0])

    wait_bytes(fin_out, out_send)
    wait_bytes(out_ref.at[0], out_recv)


def on_device(stream, norm_gain, qkv_weight, out_weight, stale_kv):
    tokens, width = stream.shape
    stale = stale_kv.reshape(tokens, 2 * HEAD)
    any_spec = pl.BlockSpec(memory_space=pl.ANY)
    bf16 = jnp.bfloat16
    dma = pltpu.SemaphoreType.DMA
    out, fresh = pl.pallas_call(
        kernel,
        out_shape=(
            jax.ShapeDtypeStruct((1, SHARD, width), bf16),
            jax.ShapeDtypeStruct((tokens, 2 * HEAD), bf16),
        ),
        in_specs=[any_spec] * 5,
        out_specs=(any_spec, any_spec),
        scratch_shapes=[
            pltpu.VMEM((width, width), bf16),
            pltpu.VMEM((width, 3 * HEAD), bf16),
            pltpu.VMEM((1, width), jnp.float32),
            pltpu.VMEM((tokens, 2 * HEAD), bf16),
            pltpu.VMEM((CHUNKS, SEQS, CHUNK, HEAD), bf16),
            pltpu.VMEM((CHUNKS, CHUNK, width), bf16),
            pltpu.VMEM((CHUNKS, CHUNK, width), bf16),
            pltpu.VMEM((CHUNKS, CHUNK, HEAD), bf16),
            pltpu.VMEM((tokens, 2 * HEAD), bf16),
            pltpu.VMEM((SEQS, SHARD, HEAD), bf16),
            pltpu.VMEM((SHARD, width), bf16),
            pltpu.VMEM((SHARD, width), bf16),
            dma((4,)),
            dma((len(GATHER),)),
            dma((SEQS,)),
            dma,
            dma((CHUNKS,)),
            dma((CHUNKS,)),
            dma((CHUNKS,)),
            dma((CHUNKS,)),
            dma,
            dma,
            dma,
            dma,
            dma((CHUNKS,)),
        ],
        compiler_params=pltpu.CompilerParams(
            collective_id=0, has_side_effects=True, vmem_limit_bytes=48 * 1024 * 1024
        ),
        name="sections",
    )(stream.reshape(CHUNKS, CHUNK, width), norm_gain, qkv_weight, out_weight, stale)
    return out, fresh.reshape(1, tokens, 1, 2 * HEAD)


def solution(mesh):
    return jax.shard_map(
        on_device,
        mesh=mesh,
        in_specs=(
            P(),
            P("sec", None),
            P("sec", None, "seq"),
            P("sec", "seq", None),
            P("sec", None, "seq", None),
        ),
        out_specs=(P("sec", "seq", None), P("sec", None, "seq", None)),
        check_vma=False,
    )
```

time: 2380 us -> 388 us (0.16)
  waiting for transfers between devices: 1640 us -> 0 us
  blocking collectives: 523 us -> 0 us
  Pallas kernels: 0 us -> 380 us
  matrix products: 93.7 us -> 0 us
  other arithmetic: 58.4 us -> 0 us
  starting transfers between devices: 24.4 us -> 0 us
    reduce_scatter x19 -> x0, waiting for transfers between devices: 1260 us -> none  [step_fn(): lax.psum_scatter(jnp.dot(context, weight_out, preferred_element_type=jnp....]
    all_gather x19 -> x0, blocking collectives: 523 us -> none  [step_fn(): whole_out = lax.all_gather(output_rows, 'seq', axis=0, tiled=True)]
    ppermute x19 -> x0, waiting for transfers between devices: 386 us -> none  [from_behind(): return lax.ppermute(value, axis, pairs)]
    pallas_call x0 -> x1, Pallas kernels: none -> 380 us  [on_device(): pl.pallas_call(kernel, out_shape=(jax.ShapeDtypeStruct((1, SHARD, width),...]
    dot_general x114 -> x0, matrix products: 93.7 us -> none  [the longest x19 36.5 us: project(): jnp.dot(piece, weight_qkv, preferred_element_type=jnp.float32)]
    reduce_sum x38 -> x0, other arithmetic: 32.1 us -> none  [the longest x19 25.1 us: normalize(): meansq = jnp.mean(x_float * x_float, axis=-1, keepdims=True)]
    ppermute x19 -> x0, starting transfers between devices: 24.3 us -> none  [from_behind(): return lax.ppermute(value, axis, pairs)]
  transfers between devices with their start and end apart: 38 -> 0, of which waited for: 38 -> 0; matrix products, arithmetic and copies ran while one was open for 0% -> 0% of each run, Pallas kernels for 0% -> 0%
where the time goes in v1:
time: 388 us
  Pallas kernels  380 us (98%)
  local copies, waits for them, and re-layouts  7.04 us (2%)
    pallas_call x1, Pallas kernels, on_device(): pl.pallas_call(kernel, out_shape=(jax.ShapeDtypeStruct((1, SHARD, width),...  380 us

profile of v1, /device:TPU:255, one launch (start us, length us, event | category | flops | bytes accessed | tf_op | source)
XLA Modules:
  0.0 388.0 jit_solution(10803633980722683651)
XLA Ops:
  0.6 0.0 copy-start
  0.6 1.6 copy-done
  2.2 0.0 copy-start.1
  2.2 1.4 copy-done.1
  3.6 0.0 copy-start.2
  3.6 1.0 copy-done.2
  4.7 0.0 copy-start.3
  4.7 0.9 copy-done.3
  5.6 0.0 copy-start.4
  5.6 0.7 copy-done.4
  6.3 380.3 %sections.1 = (bf16[1,32,2048]{2,1,0:T(8,128)(2,1)S(1)}, bf16[512,256]{1,0:T(8,128)(2,1)S(1)}) custom-call(bf16[4,128,2048]{2,1,0:T(8,128)(2,1)S(1)} %bitcast.3, f32[1,2048]{1,0:T(1,128)S(1)} %copy-done.4, bf16[1,2048,384]{2,1,0:T(8,128)(2,1)S(1)} %copy-done.1, bf16[1,128,2048]{2,1,0:T(8,128)(2,1)S(1)} %copy-done.2, bf16[512,256]{1,0:T(8,128)(2,1)S(1)} %bitcast.4), custom_call_target="tpu_custom_call" | custom-call | tf_op jit(solution)/shard_map/sections/pallas_call | solution.py:367
  386.6 0.7 copy.9
  387.3 0.7 copy.10
Async XLA Ops:
  0.6 1.6 copy-start
  2.2 1.4 copy-start.1
  3.6 1.0 copy-start.2
  4.7 0.9 copy-start.3
  5.6 0.7 copy-start.4
